TPU v7x, 32 devices: a whole 2x2x4 slice. The times are simulated.
32 devices in a mesh: groups: 2 (over x), seq: 8 (over z, y), head: 2 (over core).
Axes of the slice: x: 2, y: 2, z: 4, core: 2. Of those that a mesh axis runs over, the one named last changes fastest.
Arguments:
- byte_ids: int32 [8192], P(('groups', 'seq')), parts along dimension 0, may hold values from 0 to 255
- embed_table: bfloat16 [256, 1024], P(None, 'head'), may hold values from -6 to 6
- gains: float32 [2, 1024], replicated, may hold values from 0.1 to 1.9
- conv_weight: bfloat16 [2, 3, 1024, 1024], P(None, None, None, 'head'), may hold values from -0.109375 to 0.109375
- conv_bias: float32 [2, 1024], P(None, 'head'), may hold values from -3 to 3
- qkv_weight: bfloat16 [3, 1024, 2048], P(None, None, 'head'), may hold values from -5 to 5
Outputs:
- context: bfloat16 [1024, 2048], P(('groups', 'seq'), 'head'), parts along dimension 0
There are 2 independent parts, one for each index of `groups`. A program takes and returns all parts, laid end to end along the dimension named above; an argument that names none is the same for every part. Nothing has to cross between parts.
All inputs are finite; a program needn't handle non-finite values.
Results may differ from a plain program's by a relative error of at most 0.0173.
The roundings to bfloat16 on the way count: a program that leaves them out, or rounds other values in their place, can miss the bound.
Values may be sent and summed in bfloat16 or wider, within the bound.
A program may use at most 128 MiB of HBM per device.

v0:
```python
import jax
import jax.numpy as jnp
from jax import lax
from jax.sharding import PartitionSpec as P

D = 1024
HEAD_SIZE = 64
LAYERS = 2
DILATION_FIRST = 1024
DILATION_SECOND = 2048
POOL = 8


epsilon = 1e-05


def activate(stream, gain_row, squares):
    rescale = lax.rsqrt(squares / D + epsilon)
    return jax.nn.gelu(stream * rescale[:, None] * gain_row[None, :], approximate=False).astype(
        jnp.bfloat16
    )


def slide(rows, amount):
    padding = jnp.zeros((abs(amount), rows.shape[1]), rows.dtype)
    if amount > 0:
        return jnp.concatenate([padding, rows[:-amount]], axis=0)
    return jnp.concatenate([rows[-amount:], padding], axis=0)


def attend(running, key_rows, value_rows, queries, query_pos, key_pos):
    row_max, totals, weighted = running
    heads_here = queries.shape[1]
    key_count = key_rows.shape[0]
    key_heads = key_rows.reshape(key_count, heads_here, HEAD_SIZE)
    value_heads = value_rows.reshape(key_count, heads_here, HEAD_SIZE)
    scores = jnp.einsum(
        "qhd,khd->hqk", queries, key_heads, preferred_element_type=jnp.float32
    ) * HEAD_SIZE ** (-0.5)
    visible = key_pos[None, None, :] <= query_pos[None, :, None]
    masked = jnp.where(visible, scores, -1e30)
    new_max = jnp.maximum(row_max, jnp.max(masked, axis=2))
    powers = jnp.where(visible, jnp.exp(masked - new_max[:, :, None]), 0.0)
    totals = jnp.sum(powers, axis=2)
    weighted = jnp.einsum("hqk,khd->hqd", powers, value_heads.astype(jnp.float32))
    return (new_max, totals, weighted)


def local(byte_ids, embed_table, gains, conv_weight, conv_bias, qkv_weight):
    row_count = byte_ids.shape[0]
    width_half = embed_table.shape[1]
    seq_count = lax.axis_size("seq")
    seq_place = lax.axis_index("seq")
    stride_cells = DILATION_FIRST // seq_count
    stride_pooled = stride_cells // POOL
    pooled_rows = row_count // POOL
    all_ids = lax.all_gather(byte_ids, "seq", axis=0, tiled=True)
    all_ids = all_ids.reshape(-1, seq_count, stride_cells)
    local_ids = lax.dynamic_slice_in_dim(all_ids, seq_place, 1, 1).reshape(row_count)
    vocab_ids = jnp.arange(embed_table.shape[0], dtype=jnp.int32)
    one_hot = (local_ids[:, None] == vocab_ids[None, :]).astype(jnp.bfloat16)
    stream = jnp.dot(one_hot, embed_table, preferred_element_type=jnp.float32)
    dilation_list = (DILATION_FIRST, DILATION_SECOND)
    for layer_index in range(LAYERS):
        local_step = dilation_list[layer_index] // DILATION_FIRST * stride_cells
        whole_rows = lax.all_gather(stream, "head", axis=1, tiled=True)
        active = activate(whole_rows, gains[layer_index], jnp.sum(whole_rows * whole_rows, axis=1))
        behind = slide(active, local_step)
        in_front = slide(active, -local_step)
        mixed = jnp.dot(behind, conv_weight[layer_index, 0], preferred_element_type=jnp.float32)
        mixed = mixed + jnp.dot(
            active, conv_weight[layer_index, 1], preferred_element_type=jnp.float32
        )
        mixed = mixed + jnp.dot(
            in_front, conv_weight[layer_index, 2], preferred_element_type=jnp.float32
        )
        stream = stream + mixed + conv_bias[layer_index][None, :]
    pooled = jnp.mean(stream.reshape(pooled_rows, POOL, width_half), axis=1).astype(jnp.bfloat16)
    pooled_full = lax.all_gather(pooled, "head", axis=1, tiled=True)
    heads_here = qkv_weight.shape[2] // HEAD_SIZE
    queries = jnp.dot(pooled_full, qkv_weight[0], preferred_element_type=jnp.float32).astype(
        jnp.bfloat16
    )
    queries = queries.reshape(pooled_rows, heads_here, HEAD_SIZE)
    period = DILATION_FIRST // POOL

    def key_places(offset, count):
        rows_here = offset + jnp.arange(count, dtype=jnp.int32)
        source = rows_here // pooled_rows
        inner = rows_here % pooled_rows
        return inner // stride_pooled * period + source * stride_pooled + inner % stride_pooled

    query_pos = key_places(seq_place * pooled_rows, pooled_rows)
    start_state = (
        jnp.full((heads_here, pooled_rows), -1e30, jnp.float32),
        jnp.zeros((heads_here, pooled_rows), jnp.float32),
        jnp.zeros((heads_here, pooled_rows, HEAD_SIZE), jnp.float32),
    )
    key_rows = jnp.dot(pooled_full, qkv_weight[1], preferred_element_type=jnp.float32).astype(
        jnp.bfloat16
    )
    value_rows = jnp.dot(pooled_full, qkv_weight[2], preferred_element_type=jnp.float32).astype(
        jnp.bfloat16
    )
    pieces = (
        lax.all_gather(key_rows, "seq", axis=0, tiled=True),
        lax.all_gather(value_rows, "seq", axis=0, tiled=True),
    )
    row_max, totals, weighted = attend(
        start_state,
        pieces[0],
        pieces[1],
        queries,
        query_pos,
        key_places(jnp.int32(0), pieces[0].shape[0]),
    )
    out_width = heads_here * HEAD_SIZE
    context = (weighted / totals[:, :, None]).transpose(1, 0, 2).reshape(pooled_rows, out_width)
    context = context.astype(jnp.bfloat16)
    block_count = pooled_rows // stride_pooled
    fan_count = seq_count // block_count
    target = seq_place * stride_pooled // pooled_rows
    picked_dilation = jnp.arange(fan_count, dtype=jnp.int32) == target
    sectioned = jnp.where(
        picked_dilation[None, :, None, None],
        context.reshape(block_count, 1, stride_pooled, out_width),
        jnp.zeros((), jnp.bfloat16),
    )
    sectioned = sectioned.reshape(seq_count * stride_pooled, out_width)
    arrived = lax.all_to_all(sectioned, "seq", split_axis=0, concat_axis=0, tiled=True)
    arrived = arrived.reshape(seq_count, stride_pooled, out_width)
    context = lax.dynamic_slice_in_dim(arrived, seq_place % fan_count * block_count, block_count, 0)
    context = context.reshape(pooled_rows, out_width)
    return context


def solution(mesh):
    placed = (
        P(("groups", "seq")),
        P(None, "head"),
        P(),
        P(None, None, None, "head"),
        P(None, "head"),
        P(None, None, "head"),
    )
    return jax.shard_map(
        local, mesh=mesh, in_specs=placed, out_specs=P(("groups", "seq"), "head"), check_vma=False
    )
```

profile of v0, /device:TPU:0, one launch (start us, length us, event | category | flops | bytes accessed | tf_op | source)
XLA Modules:
  0.0 191.9 jit_solution(12096868458623567444)
XLA Ops:
  6.6 28.1 %all-gather = s32[8,1,512]{2,1,0:T(1,128)S(1)} all-gather(s32[1,1,512]{2,1,0:T(1,128)} %bitcast.72), channel_id=1, replica_groups=mesh['groups'=2,'seq'=8,'head'=2] {'seq'}, dimensions={0}, use_global_device_ids=true | all-gather | bytes 18432 | tf_op jit(solution)/shard_map/all_gather | solution.py:57
  34.6 1.3 fusion.73
  36.0 0.0 all-gather.6.cloned.1.call-update
  36.0 0.0 all-gather.8.cloned.1.call-start
  36.0 0.0 copy-done.7
  36.1 9.9 %all-gather.6.cloned.1.call-done = f32[512,1024]{1,0:T(8,128)} async-done(((f32[512,512]{1,0:T(8,128)}), f32[512,1024]{1,0:T(8,128)}) %all-gather.6.cloned.1.call-update) | async-done | bytes 2097168 | tf_op jit(solution)/shard_map/all_gather | solution.py:66
  46.0 2.0 %multiply_reduce_fusion.1 = f32[512]{0:T(512)S(1)} fusion(f32[512,1024]{1,0:T(8,128)} %all-gather.6.cloned.1.call-done), kind=kLoop, calls=%fused_computation.48 | loop fusion | flops 1048064 | bytes 2099200 | tf_op jit(solution)/shard_map/reduce_sum | solution.py:67
  48.0 0.3 copy-done.2
  48.2 5.1 %fusion.2 = bf16[512,1024]{1,0:T(8,128)(2,1)S(1)} fusion(f32[512,1024]{1,0:T(8,128)S(1)} %copy-done.2, f32[1024]{0:T(1024)S(1)} %bitcast.68, f32[512]{0:T(512)S(1)} %add_rsqrt_fusion.1), kind=kLoop, calls=%fused_computation.4 | loop fusion | flops 35127296 | bytes 3151872 | tf_op jit(solution)/shard_map/convert_element_type | solution.py:19
  53.3 0.2 fusion.99
  53.5 0.0 copy-done.5
  53.5 0.7 fusion.56
  54.2 0.7 convolution_add_fusion.3
  54.9 0.5 copy-done.1
  55.4 1.7 fusion.34
  57.1 0.0 all-gather.8.cloned.1.call-update
  57.1 0.0 all-gather.10.cloned.1.call-start
  57.2 11.9 %all-gather.8.cloned.1.call-done = f32[512,1024]{1,0:T(8,128)} async-done(((f32[512,512]{1,0:T(8,128)}), f32[512,1024]{1,0:T(8,128)}) %all-gather.8.cloned.1.call-update) | async-done | bytes 2097168 | tf_op jit(solution)/shard_map/all_gather | solution.py:66
  69.1 2.0 %multiply_reduce_fusion = f32[512]{0:T(512)S(1)} fusion(f32[512,1024]{1,0:T(8,128)} %all-gather.8.cloned.1.call-done), kind=kLoop, calls=%fused_computation.33 | loop fusion | flops 1048064 | bytes 2099200 | tf_op jit(solution)/shard_map/reduce_sum | solution.py:67
  71.0 0.3 copy-done.3
  71.3 5.1 %fusion.5 = bf16[512,1024]{1,0:T(8,128)(2,1)S(1)} fusion(f32[512,1024]{1,0:T(8,128)S(1)} %copy-done.3, f32[1024]{0:T(1024)S(1)} %bitcast.67, f32[512]{0:T(512)S(1)} %add_rsqrt_fusion), kind=kLoop, calls=%fused_computation.7 | loop fusion | flops 35127296 | bytes 3151872 | tf_op jit(solution)/shard_map/convert_element_type | solution.py:19
  76.3 0.1 fusion.98
  76.4 1.9 %fusion.52 = f32[512,512]{1,0:T(8,128)S(1)} fusion(bf16[2,3,1024,512]{3,2,1,0:T(8,128)(2,1)} %param.9, bf16[256,1024]{1,0:T(8,128)(2,1)S(1)} %get-tuple-element.6), kind=kOutput, calls=%fused_computation.74 | convolution fusion | flops 536870912 | bytes 2621440 | tf_op jit(solution)/shard_map/dot_general | solution.py:70
  78.4 2.0 %convolution_add_fusion.1 = f32[512,512]{1,0:T(8,128)S(1)} fusion(f32[512,512]{1,0:T(8,128)S(1)} %fusion.52, bf16[512,1024]{1,0:T(8,128)(2,1)S(1)} %fusion.5, bf16[2,3,1024,512]{3,2,1,0:T(8,128)(2,1)} %param.9), kind=kOutput, calls=%fused_computation.58 | convolution fusion | flops 537133056 | bytes 4194304 | tf_op jit(solution)/shard_map/dot_general | solution.py:71
  80.4 2.2 %fusion.37 = f32[64,512]{1,0:T(8,128)S(1)} fusion(f32[512,512]{1,0:T(8,128)S(1)} %copy-done.4, f32[512,512]{1,0:T(8,128)S(1)} %convolution_add_fusion.1, bf16[2,3,1024,512]{3,2,1,0:T(8,128)(2,1)} %param.9, bf16[256,1024]{1,0:T(8,128)(2,1)S(1)} %get-tuple-element.5, f32[512]{0:T(512)S(1)} %bitcast.73), kind=kOutput, calls=%fused_computation.65 | convolution fusion | flops 537886720 | bytes 3803136 | tf_op jit(solution)/shard_map/dot_general | solution.py:74
  82.6 1.9 all_gather.21
  84.5 2.7 %fusion.42 = bf16[64,1024]{1,0:T(8,128)(2,1)} fusion(bf16[64,1024]{1,0:T(8,128)(2,1)S(1)} %all_gather.21, bf16[3,1024,1024]{2,1,0:T(8,128)(2,1)} %param.11), kind=kOutput, calls=%fused_computation.68 | convolution fusion | flops 134283264 | bytes 2359296 | tf_op jit(solution)/shard_map/dot_general | solution.py:99
  87.2 0.0 all-gather.10.cloned.1.call-update
  87.3 0.2 all-gather.12.cloned.1.call-start
  87.5 2.7 %fusion.45 = bf16[64,1024]{1,0:T(8,128)(2,1)} fusion(bf16[64,1024]{1,0:T(8,128)(2,1)S(1)} %all_gather.21, bf16[3,1024,1024]{2,1,0:T(8,128)(2,1)} %param.11), kind=kOutput, calls=%fused_computation.69 | convolution fusion | flops 134283264 | bytes 2359296 | tf_op jit(solution)/shard_map/dot_general | solution.py:102
  90.2 0.0 all-gather.12.cloned.1.call-update
  90.3 0.1 broadcast_in_dim.56
  90.4 0.1 broadcast_compare_fusion
  90.5 2.1 %fusion.39 = bf16[64,1024]{1,0:T(8,128)(2,1)S(1)} fusion(bf16[64,1024]{1,0:T(8,128)(2,1)S(1)} %all_gather.21, bf16[3,1024,1024]{2,1,0:T(8,128)(2,1)} %param.11), kind=kOutput, calls=%fused_computation.67 | convolution fusion | flops 134283264 | bytes 2359296 | tf_op jit(solution)/shard_map/dot_general | solution.py:81
  92.6 0.9 reshape.205
  93.5 35.3 %all-gather.10.cloned.1.call-done = bf16[512,1024]{1,0:T(8,128)(2,1)} async-done(((bf16[64,1024]{1,0:T(8,128)(2,1)}), bf16[512,1024]{1,0:T(8,128)(2,1)}) %all-gather.10.cloned.1.call-update) | async-done | bytes 1048592 | tf_op jit(solution)/shard_map/all_gather | solution.py:106
  128.7 1.5 copy.14
  130.2 1.5 fusion.29
  131.7 0.7 fusion.30
  132.4 37.2 %all-gather.12.cloned.1.call-done = bf16[512,1024]{1,0:T(8,128)(2,1)} async-done(((bf16[64,1024]{1,0:T(8,128)(2,1)}), bf16[512,1024]{1,0:T(8,128)(2,1)}) %all-gather.12.cloned.1.call-update) | async-done | bytes 1048592 | tf_op jit(solution)/shard_map/all_gather | solution.py:107
  169.7 1.5 copy.16
  171.2 0.7 fusion.49
  171.9 0.2 copy.17
  172.1 0.2 convert_element_type.37
  172.3 0.8 bitcast_select_fusion
  173.0 3.4 %all-to-all-start = ((bf16[8,16,1024]{2,1,0:T(8,128)(2,1)}), bf16[8,16,1024]{2,1,0:T(8,128)(2,1)S(1)}, u32[]{:S(2)}, u32[]{:S(2)}) async-start(bf16[8,16,1024]{2,1,0:T(8,128)(2,1)} %bitcast_select_fusion), calls=%async_computation | async-start | bytes 524288 | tf_op jit(solution)/shard_map/all_to_all | solution.py:130
  176.5 8.3 %all-to-all-done = bf16[8,16,1024]{2,1,0:T(8,128)(2,1)S(1)} async-done(((bf16[8,16,1024]{2,1,0:T(8,128)(2,1)}), bf16[8,16,1024]{2,1,0:T(8,128)(2,1)S(1)}, u32[]{:S(2)}, u32[]{:S(2)}) %all-to-all-start) | async-done | bytes 262176 | tf_op jit(solution)/shard_map/all_to_all | solution.py:130
  184.7 0.7 constant_dynamic-slice_fusion
  (23 shorter events, 0.1 us)
Async XLA Ops:
  6.5 28.1 %copy-start = (bf16[256,512]{1,0:T(8,128)(2,1)S(1)}, bf16[256,512]{1,0:T(8,128)(2,1)}, u32[]{:S(2)}) copy-start(bf16[256,512]{1,0:T(8,128)(2,1)} %param.7) | copy-start | bytes 786436
  6.5 29.5 %copy-start.7 = (f32[2,512]{1,0:T(2,128)S(1)}, f32[2,512]{1,0:T(2,128)}, u32[]{:S(2)}) copy-start(f32[2,512]{1,0:T(2,128)} %param.10) | copy-start | bytes 12292
  6.5 29.5 %copy-start.6 = (f32[2,1024]{1,0:T(2,128)S(1)}, f32[2,1024]{1,0:T(2,128)}, u32[]{:S(2)}) copy-start(f32[2,1024]{1,0:T(2,128)} %param.8) | copy-start | bytes 24580
  6.5 39.5 %all-gather.6.cloned.1.call-start = ((), (), s32[]{:S(2)}) async-start(), calls=%async_computation.1 | async-start | bytes 3145728 | tf_op jit(solution)/shard_map/all_gather | solution.py:66
  36.0 33.1 %all-gather.8.cloned.1.call-start = ((), (), s32[]{:S(2)}) async-start(), calls=%async_computation.2 | async-start | bytes 3145728 | tf_op jit(solution)/shard_map/all_gather | solution.py:66
  46.0 2.2 %copy-start.2 = (f32[512,1024]{1,0:T(8,128)S(1)}, f32[512,1024]{1,0:T(8,128)}, u32[]{:S(2)}) copy-start(f32[512,1024]{1,0:T(8,128)} %all-gather.6.cloned.1.call-done) | copy-start | bytes 6291460
  48.2 5.3 %copy-start.5 = (bf16[2,3,1024,512]{3,2,1,0:T(8,128)(2,1)S(1)}, bf16[2,3,1024,512]{3,2,1,0:T(8,128)(2,1)}, u32[]{:S(2)}) copy-start(bf16[2,3,1024,512]{3,2,1,0:T(8,128)(2,1)} %param.9) | copy-start | bytes 18874372
  54.2 1.2 copy-start.1
  57.1 71.6 %all-gather.10.cloned.1.call-start = ((), (), s32[]{:S(2)}) async-start(), calls=%async_computation.3 | async-start | bytes 1179648 | tf_op jit(solution)/shard_map/all_gather | solution.py:106
  69.1 2.2 %copy-start.3 = (f32[512,1024]{1,0:T(8,128)S(1)}, f32[512,1024]{1,0:T(8,128)}, u32[]{:S(2)}) copy-start(f32[512,1024]{1,0:T(8,128)} %all-gather.8.cloned.1.call-done) | copy-start | bytes 6291460
  78.4 2.0 %copy-start.4 = (f32[512,512]{1,0:T(8,128)S(1)}, f32[512,512]{1,0:T(8,128)}, u32[]{:S(2)}) copy-start(f32[512,512]{1,0:T(8,128)} %fusion.34) | copy-start | bytes 3145732
  87.3 82.4 %all-gather.12.cloned.1.call-start = ((), (), s32[]{:S(2)}) async-start(), calls=%async_computation.4 | async-start | bytes 1179648 | tf_op jit(solution)/shard_map/all_gather | solution.py:107
  173.0 11.7 %all-to-all-start = ((bf16[8,16,1024]{2,1,0:T(8,128)(2,1)}), bf16[8,16,1024]{2,1,0:T(8,128)(2,1)S(1)}, u32[]{:S(2)}, u32[]{:S(2)}) async-start(bf16[8,16,1024]{2,1,0:T(8,128)(2,1)} %bitcast_select_fusion), calls=%async_computation | async-start | bytes 524288 | tf_op jit(solution)/shard_map/all_to_all | solution.py:130
Sparse Core Ops, SparseCore 0:
  36.1 9.8 all-gather.5
  57.3 11.7 all-gather.7
  87.4 41.3 all-gather.9
  130.7 38.8 all-gather.11
where the time goes:
time: 192 us
  waiting for transfers between devices  103 us (54%)
  blocking collectives  30 us (16%)
  matrix products  20.3 us (11%)
  other arithmetic  15.7 us (8%)
  between operations  13.4 us (7%)
  local copies, waits for them, and re-layouts  6.31 us (3%)
  starting transfers between devices  3.72 us (2%)
    all_gather x1, waiting for transfers between devices, local(): lax.all_gather(value_rows, 'seq', axis=0, tiled=True)  37.2 us
    all_gather x1, waiting for transfers between devices, local(): lax.all_gather(key_rows, 'seq', axis=0, tiled=True)  35.3 us
    all_gather x1, blocking collectives, local(): all_ids = lax.all_gather(byte_ids, 'seq', axis=0, tiled=True)  28.1 us
    all_gather x2, waiting for transfers between devices, local(): whole_rows = lax.all_gather(stream, 'head', axis=1, tiled=True)  21.8 us
    convert_element_type x2, other arithmetic, activate(): jax.nn.gelu(stream * rescale[:, None] * gain_row[None, :], approximate=Fa...  10.1 us
    all_to_all x1, waiting for transfers between devices, local(): lax.all_to_all(sectioned, 'seq', split_axis=0, concat_axis=0, tiled=True)  8.27 us
    reduce_sum x2, other arithmetic, local(): jnp.sum(whole_rows * whole_rows, axis=1)  3.9 us
    dot_general x2, matrix products, local(): jnp.dot(in_front, conv_weight[layer_index, 2], preferred_element_type=jnp...  3.87 us
  transfers between devices with their start and end apart: 5, of which 5 were waited for; matrix products, arithmetic and copies ran while one was open for 5% of the time, Pallas kernels for 0%

commit v1 on v0

v1 whole, which is shorter than its diff:
```python
import functools

import jax
import jax.numpy as jnp
from jax import lax
from jax.experimental import pallas as pl
from jax.experimental.pallas import tpu as pltpu
from jax.sharding import PartitionSpec as P

HEAD_SIZE = 64
LAYERS = 2
DILATION_FIRST = 1024
POOL = 8
EPSILON = 1e-05
MESH = pl.DeviceIdType.MESH
F32 = jnp.float32
BF16 = jnp.bfloat16

ERF_P = (
    -2.72614225801306e-10,
    2.77068142495902e-08,
    -2.10102402082508e-06,
    -5.69250639462346e-05,
    -7.34990630326855e-04,
    -2.95459980854025e-03,
    -1.60960333262415e-02,
)
ERF_Q = (
    -1.45660718464996e-05,
    -2.13374055278905e-04,
    -1.68282697438203e-03,
    -7.37332916720468e-03,
    -1.42647390514189e-02,
)


def gelu(v):
    t = jnp.clip(v * 0.7071067811865476, -4.0, 4.0)
    t2 = t * t
    p = jnp.full_like(t2, ERF_P[0])
    for coefficient in ERF_P[1:]:
        p = p * t2 + coefficient
    q = jnp.full_like(t2, ERF_Q[0])
    for coefficient in ERF_Q[1:]:
        q = q * t2 + coefficient
    return 0.5 * v * (1.0 + t * p / q)


def inner_of(seq_count):
    inner = 1
    while (inner * 2) * (inner * 2) <= seq_count:
        inner *= 2
    return inner


def kernel(
    seq_count,
    ids_ref,
    table_ref,
    gains_ref,
    conv_hbm,
    bias_ref,
    qkv_hbm,
    out_ref,
    ids_buf,
    table_all,
    act_table,
    act,
    stream,
    acc,
    pooled_all,
    query_buf,
    key_buf,
    value_buf,
    conv_w,
    qkv_w,
    load_sem,
    ids_send,
    ids_recv,
    table_send,
    table_recv,
    stream_send,
    stream_recv,
    own_send,
    forward_send,
    core_send,
    block_recv,
    core_recv,
):
    pieces, _, cells = ids_ref.shape
    rows = pieces * cells
    vocab, half = table_ref.shape
    pooled_rows = rows // POOL
    inner = inner_of(seq_count)
    outer = seq_count // inner
    seq = lax.axis_index("seq")
    head = lax.axis_index("head")
    other = 1 - head
    outer_place = seq // inner
    inner_place = lax.rem(seq, inner)

    loads = [
        pltpu.make_async_copy(conv_hbm.at[0], conv_w.at[0], load_sem.at[0]),
        pltpu.make_async_copy(conv_hbm.at[1], conv_w.at[1], load_sem.at[1]),
        pltpu.make_async_copy(qkv_hbm, qkv_w, load_sem.at[2]),
    ]
    for load in loads:
        load.start()

    barrier = pltpu.get_barrier_semaphore()
    pl.semaphore_signal(barrier, inc=1, device_id={"head": other}, device_id_type=MESH)
    for step in range(1, seq_count):
        pl.semaphore_signal(
            barrier,
            inc=1,
            device_id={"seq": lax.rem(seq + step, seq_count)},
            device_id_type=MESH,
        )
    pl.semaphore_wait(barrier, seq_count)

    for piece in range(pieces):
        number = seq * pieces + piece
        target = lax.rem(number, seq_count)
        slot = number // seq_count

        @pl.when(target != seq)
        def _():
            pltpu.make_async_remote_copy(
                src_ref=ids_ref.at[piece],
                dst_ref=ids_buf.at[slot],
                send_sem=ids_send.at[piece],
                recv_sem=ids_recv.at[slot],
                device_id={"seq": target},
                device_id_type=MESH,
            ).start()

        @pl.when(target == seq)
        def _():
            pltpu.make_async_copy(
                ids_ref.at[piece], ids_buf.at[slot], ids_recv.at[slot]
            ).start()

    table_copy = pltpu.make_async_remote_copy(
        src_ref=table_ref,
        dst_ref=table_all.at[head],
        send_sem=table_send,
        recv_sem=table_recv,
        device_id={"head": other},
        device_id_type=MESH,
    )
    table_copy.start()
    table_all[head] = table_ref[...]
    table_copy.wait_recv()

    def activate(first, second, layer):
        total = jnp.sum(first * first, axis=1, keepdims=True) + jnp.sum(
            second * second, axis=1, keepdims=True
        )
        rescale = lax.rsqrt(total / (2 * half) + EPSILON)
        gain = gains_ref[layer : layer + 1, :]
        return (
            gelu(first * rescale * gain[:, :half]).astype(BF16),
            gelu(second * rescale * gain[:, half:]).astype(BF16),
        )

    CHUNK = 16
    UNROLL = 2

    @pl.loop(0, vocab // (CHUNK * UNROLL))
    def _(step):
        for part in range(UNROLL):
            place = pl.ds(pl.multiple_of((step * UNROLL + part) * CHUNK, CHUNK), CHUNK)
            first, second = activate(
                table_all[0, place, :].astype(F32), table_all[1, place, :].astype(F32), 0
            )
            act_table[place, :half] = first
            act_table[place, half:] = second

    vocab_ids = lax.broadcasted_iota(jnp.int32, (vocab, cells), 0)
    for piece in range(pieces):
        pltpu.make_async_copy(
            ids_ref.at[piece], ids_buf.at[piece], ids_recv.at[piece]
        ).wait()
        one_hot = (vocab_ids == ids_buf[piece]).astype(F32).astype(BF16)
        span = slice(piece * cells, (piece + 1) * cells)
        contract = (((0,), (0,)), ((), ()))
        stream[head, span, :] = lax.dot_general(
            one_hot, table_ref[...], contract, preferred_element_type=F32
        )
        act[span, :] = lax.dot_general(
            one_hot, act_table[...], contract, preferred_element_type=F32
        ).astype(BF16)

    def convolve(layer, step, start, stop):
        acc[start:stop, :] = (
            stream[head, start:stop, :]
            + bias_ref[layer : layer + 1, :]
            + jnp.dot(act[start:stop, :], conv_w[layer, 1], preferred_element_type=F32)
        )
        low = max(start, step)
        if low < stop:
            acc[low:stop, :] += jnp.dot(
                act[low - step : stop - step, :], conv_w[layer, 0], preferred_element_type=F32
            )
        high = min(stop, rows - step)
        if start < high:
            acc[start:high, :] += jnp.dot(
                act[start + step : high + step, :], conv_w[layer, 2], preferred_element_type=F32
            )

    PARTS = 2
    span_rows = rows // PARTS
    loads[0].wait()
    stream_copies = []
    for part in range(PARTS):
        start, stop = part * span_rows, (part + 1) * span_rows
        convolve(0, cells, start, stop)
        stream[head, start:stop, :] = acc[start:stop, :]
        copy = pltpu.make_async_remote_copy(
            src_ref=stream.at[head, pl.ds(start, span_rows)],
            dst_ref=stream.at[head, pl.ds(start, span_rows)],
            send_sem=stream_send.at[part],
            recv_sem=stream_recv.at[part],
            device_id={"head": other},
            device_id_type=MESH,
        )
        copy.start()
        stream_copies.append(copy)

    for part in range(PARTS):
        stream_copies[part].wait_recv()

        @pl.loop(0, span_rows // (CHUNK * UNROLL))
        def _(step):
            for chunk in range(UNROLL):
                place = pl.ds(
                    pl.multiple_of(part * span_rows + (step * UNROLL + chunk) * CHUNK, CHUNK),
                    CHUNK,
                )
                first, second = activate(stream[0, place, :], stream[1, place, :], 1)
                act[place, :half] = first
                act[place, half:] = second

    loads[1].wait()
    for part in range(PARTS):
        convolve(1, 2 * cells, part * span_rows, (part + 1) * span_rows)
    pooled_all[head, seq] = jnp.mean(
        acc[...].reshape(pooled_rows, POOL, half), axis=1
    ).astype(BF16)

    def push(block, device, send, recv):
        copy = pltpu.make_async_remote_copy(
            src_ref=pooled_all.at[head, block],
            dst_ref=pooled_all.at[head, block],
            send_sem=send,
            recv_sem=recv,
            device_id=device,
            device_id_type=MESH,
        )
        copy.start()
        return copy

    def arrived(block):
        pltpu.make_async_remote_copy(
            src_ref=pooled_all.at[head, block],
            dst_ref=pooled_all.at[head, block],
            send_sem=block_recv.at[block],
            recv_sem=block_recv.at[block],
            device_id={"head": other},
            device_id_type=MESH,
        ).wait_recv()

    sent = []
    for step in range(1, inner):
        target = outer_place * inner + lax.rem(inner_place + step, inner)
        sent.append(
            push(seq, {"seq": target}, forward_send.at[step - 1], block_recv.at[seq])
        )
    for step in range(1, outer):
        target = lax.rem(outer_place + step, outer) * inner + inner_place
        sent.append(push(seq, {"seq": target}, own_send.at[step - 1], block_recv.at[seq]))
    sent.append(push(seq, {"head": other}, core_send.at[0], core_recv.at[seq]))
    count = 1
    for step in range(1, outer):
        block = lax.rem(outer_place + outer - step, outer) * inner + inner_place
        arrived(block)
        for aside in range(1, inner):
            target = outer_place * inner + lax.rem(inner_place + aside, inner)
            sent.append(
                push(
                    block,
                    {"seq": target},
                    forward_send.at[step * (inner - 1) + aside - 1],
                    block_recv.at[block],
                )
            )
        sent.append(push(block, {"head": other}, core_send.at[count], core_recv.at[block]))
        count += 1
    for step in range(outer):
        for aside in range(1, inner):
            block = lax.rem(outer_place + outer - step, outer) * inner + lax.rem(
                inner_place + inner - aside, inner
            )
            arrived(block)
            sent.append(push(block, {"head": other}, core_send.at[count], core_recv.at[block]))
            count += 1
    for block in range(seq_count):
        pltpu.make_async_remote_copy(
            src_ref=pooled_all.at[other, block],
            dst_ref=pooled_all.at[other, block],
            send_sem=core_recv.at[block],
            recv_sem=core_recv.at[block],
            device_id={"head": other},
            device_id_type=MESH,
        ).wait_recv()

    loads[2].wait()
    whole = seq_count * pooled_rows
    width = qkv_w.shape[2]
    stride = cells // POOL
    period = DILATION_FIRST // POOL

    def position(place):
        source = place // pooled_rows
        within = lax.rem(place, pooled_rows)
        return within // stride * period + source * stride + lax.rem(within, stride)

    key_pos = position(lax.broadcasted_iota(jnp.int32, (pooled_rows, whole), 1))
    query_pos = seq * pooled_rows + lax.broadcasted_iota(jnp.int32, (pooled_rows, whole), 0)
    pick = (key_pos == query_pos).astype(F32).astype(BF16)
    sides = [pooled_all[side].reshape(whole, half) for side in range(2)]
    picked = [
        jnp.dot(pick, side, preferred_element_type=F32).astype(BF16) for side in sides
    ]
    TILE = 256
    for column in range(0, width, TILE):
        columns = slice(column, column + TILE)
        query_buf[:, columns] = (
            jnp.dot(picked[0], qkv_w[0, :half, columns], preferred_element_type=F32)
            + jnp.dot(picked[1], qkv_w[0, half:, columns], preferred_element_type=F32)
        ).astype(BF16)

    BAND = 8 * pooled_rows if seq_count % 8 == 0 else pooled_rows

    @pl.loop(0, whole // BAND)
    def _(band):
        blocks = pl.ds(band * (BAND // pooled_rows), BAND // pooled_rows)
        left = pooled_all[0, blocks].reshape(BAND, half)
        right = pooled_all[1, blocks].reshape(BAND, half)
        place = pl.ds(pl.multiple_of(band * BAND, BAND), BAND)
        for kind, target in ((1, key_buf), (2, value_buf)):
            for column in range(0, width, TILE):
                columns = slice(column, column + TILE)
                target[place, columns] = (
                    jnp.dot(left, qkv_w[kind, :half, columns], preferred_element_type=F32)
                    + jnp.dot(right, qkv_w[kind, half:, columns], preferred_element_type=F32)
                ).astype(BF16)

    PAIR = 2 * HEAD_SIZE
    lane = lax.broadcasted_iota(jnp.int32, (pooled_rows, PAIR), 1)
    left_lanes = lane < HEAD_SIZE
    visible = key_pos <= query_pos
    visible = jnp.concatenate([visible.astype(F32)] * 2, axis=0) > 0.5
    zero = jnp.zeros((pooled_rows, PAIR), F32)
    for column in range(0, width, PAIR):
        columns = slice(column, column + PAIR)
        query = query_buf[:, columns].astype(F32) * HEAD_SIZE ** (-0.5)
        stacked = jnp.concatenate(
            [jnp.where(left_lanes, query, zero), jnp.where(left_lanes, zero, query)], axis=0
        ).astype(BF16)
        scores = lax.dot_general(
            stacked, key_buf[:, columns], (((1,), (1,)), ((), ())), preferred_element_type=F32
        )
        scores = jnp.where(visible, scores, -1e30)
        top = jnp.max(scores, axis=1, keepdims=True)
        powers = jnp.where(visible, jnp.exp(scores - top), 0.0)
        total = jnp.sum(powers, axis=1, keepdims=True)
        weighted = (
            jnp.dot(powers.astype(BF16), value_buf[:, columns], preferred_element_type=F32)
            / total
        )
        out_ref[:, columns] = jnp.where(
            left_lanes, weighted[:pooled_rows], weighted[pooled_rows:]
        ).astype(BF16)

    for piece in range(pieces):
        target = lax.rem(seq * pieces + piece, seq_count)

        @pl.when(target != seq)
        def _():
            pltpu.make_async_remote_copy(
                src_ref=ids_ref.at[piece],
                dst_ref=ids_buf.at[0],
                send_sem=ids_send.at[piece],
                recv_sem=ids_recv.at[0],
                device_id={"seq": target},
                device_id_type=MESH,
            ).wait_send()

    table_copy.wait_send()
    for copy in stream_copies:
        copy.wait_send()
    for copy in sent:
        copy.wait_send()


def local(byte_ids, embed_table, gains, conv_weight, conv_bias, qkv_weight):
    seq_count = lax.axis_size("seq")
    rows = byte_ids.shape[0]
    vocab, half = embed_table.shape
    depth = conv_weight.shape[2]
    cells = DILATION_FIRST // seq_count
    pieces = rows // cells
    pooled_rows = rows // POOL
    width = qkv_weight.shape[2]
    whole = seq_count * pooled_rows
    inner = inner_of(seq_count)
    outer = seq_count // inner
    dma = pltpu.SemaphoreType.DMA
    vmem = pl.BlockSpec(memory_space=pltpu.VMEM)
    hbm = pl.BlockSpec(memory_space=pl.ANY)
    return pl.pallas_call(
        functools.partial(kernel, seq_count),
        out_shape=jax.ShapeDtypeStruct((pooled_rows, width), BF16),
        in_specs=[vmem, vmem, vmem, hbm, vmem, hbm],
        out_specs=vmem,
        scratch_shapes=[
            pltpu.VMEM((pieces, 1, cells), jnp.int32),
            pltpu.VMEM((2, vocab, half), BF16),
            pltpu.VMEM((vocab, depth), BF16),
            pltpu.VMEM((rows, depth), BF16),
            pltpu.VMEM((2, rows, half), F32),
            pltpu.VMEM((rows, half), F32),
            pltpu.VMEM((2, seq_count, pooled_rows, half), BF16),
            pltpu.VMEM((pooled_rows, width), BF16),
            pltpu.VMEM((whole, width), BF16),
            pltpu.VMEM((whole, width), BF16),
            pltpu.VMEM(conv_weight.shape, BF16),
            pltpu.VMEM(qkv_weight.shape, BF16),
            dma((3,)),
            dma((pieces,)),
            dma((pieces,)),
            dma,
            dma,
            dma((2,)),
            dma((2,)),
            dma((max(outer - 1, 1),)),
            dma((max(outer * (inner - 1), 1),)),
            dma((seq_count,)),
            dma((seq_count,)),
            dma((seq_count,)),
        ],
        compiler_params=pltpu.CompilerParams(
            collective_id=0, has_side_effects=True, vmem_limit_bytes=58 * 1024 * 1024
        ),
        name="stem",
    )(
        byte_ids.reshape(pieces, 1, cells),
        embed_table,
        gains,
        conv_weight,
        conv_bias,
        qkv_weight,
    )


def solution(mesh):
    placed = (
        P(("groups", "seq")),
        P(None, "head"),
        P(),
        P(None, None, None, "head"),
        P(None, "head"),
        P(None, None, "head"),
    )
    return jax.shard_map(
        local, mesh=mesh, in_specs=placed, out_specs=P(("groups", "seq"), "head"), check_vma=False
    )
```

time: 192 us -> 38.5 us (0.20)
  waiting for transfers between devices: 103 us -> 0 us
  Pallas kernels: 0 us -> 36.6 us
  blocking collectives: 30 us -> 0 us
  matrix products: 20.3 us -> 0 us
  other arithmetic: 15.7 us -> 0 us
  between operations: 13.4 us -> 0.01 us
  local copies, waits for them, and re-layouts: 6.31 us -> 1.57 us
  starting transfers between devices: 3.72 us -> 0 us
    all_gather x4 -> x0, waiting for transfers between devices: 94.3 us -> none  [the longest x1 37.2 us: local(): lax.all_gather(value_rows, 'seq', axis=0, tiled=True)]
    pallas_call x0 -> x1, Pallas kernels: none -> 36.6 us  [local(): pl.pallas_call(functools.partial(kernel, seq_count), out_shape=jax.ShapeD...]
    all_gather x2 -> x0, blocking collectives: 30 us -> none  [the longest x1 28.1 us: local(): all_ids = lax.all_gather(byte_ids, 'seq', axis=0, tiled=True)]
    dot_general x12 -> x0, matrix products: 20.3 us -> none  [the longest x2 3.87 us: local(): jnp.dot(in_front, conv_weight[layer_index, 2], preferred_element_type=jnp...]
    convert_element_type x3 -> x0, other arithmetic: 10.1 us -> none  [the longest x2 10.1 us: activate(): jax.nn.gelu(stream * rescale[:, None] * gain_row[None, :], approximate=Fa...]
    all_to_all x1 -> x0, waiting for transfers between devices: 8.27 us -> none  [local(): lax.all_to_all(sectioned, 'seq', split_axis=0, concat_axis=0, tiled=True)]
    reduce_sum x3 -> x0, other arithmetic: 4.58 us -> none  [the longest x2 3.9 us: local(): jnp.sum(whole_rows * whole_rows, axis=1)]
    all_to_all x1 -> x0, starting transfers between devices: 3.41 us -> none  [local(): lax.all_to_all(sectioned, 'seq', split_axis=0, concat_axis=0, tiled=True)]
  transfers between devices with their start and end apart: 5 -> 0, of which waited for: 5 -> 0; matrix products, arithmetic and copies ran while one was open for 5% -> 0% of each run, Pallas kernels for 0% -> 0%
where the time goes in v1:
time: 38.5 us; the launch traced here: 38.2 us
  Pallas kernels  36.6 us (95%)
  local copies, waits for them, and re-layouts  1.57 us (4%)
    pallas_call x1, Pallas kernels, local(): pl.pallas_call(functools.partial(kernel, seq_count), out_shape=jax.ShapeD...  36.6 us
    unnamed x1, local copies, waits for them, and re-layouts  1.57 us

profile of v1, /device:TPU:0, one launch (start us, length us, event | category | flops | bytes accessed | tf_op | source)
XLA Modules:
  0.0 38.2 jit_solution(6130629398625914615)
XLA Ops:
  0.0 36.6 %stem.1 = bf16[64,1024]{1,0:T(8,128)(2,1)} custom-call(s32[4,1,128]{2,1,0:T(1,128)} %bitcast.1, bf16[256,512]{1,0:T(8,128)(2,1)} %table_ref.1, f32[2,1024]{1,0:T(2,128)} %gains_ref.1, bf16[2,3,1024,512]{3,2,1,0:T(8,128)(2,1)} %conv_hbm.1, f32[2,512]{1,0:T(2,128)} %bias_ref.1, bf16[3,1024,1024]{2,1,0:T(8,128)(2,1)} %qkv_hbm.1), custom_call_target="tpu_custom_call" | custom-call | tf_op jit(solution)/shard_map/stem/pallas_call | solution.py:422
  36.6 1.6 %copy.8 = bf16[64,1024]{1,0:T(8,128)(2,1)} copy(bf16[64,1024]{1,0:T(8,128)(2,1)} %stem.1) | data formatting | bytes 262144

commit v2 on v1

--- a/solution.py
+++ b/solution.py
@@ -81,8 +81,9 @@
     table_recv,
     stream_send,
     stream_recv,
-    own_send,
-    forward_send,
+    up_send,
+    down_send,
+    aside_send,
     core_send,
     block_recv,
     core_recv,
@@ -99,14 +100,6 @@
     outer_place = seq // inner
     inner_place = lax.rem(seq, inner)
 
-    loads = [
-        pltpu.make_async_copy(conv_hbm.at[0], conv_w.at[0], load_sem.at[0]),
-        pltpu.make_async_copy(conv_hbm.at[1], conv_w.at[1], load_sem.at[1]),
-        pltpu.make_async_copy(qkv_hbm, qkv_w, load_sem.at[2]),
-    ]
-    for load in loads:
-        load.start()
-
     barrier = pltpu.get_barrier_semaphore()
     pl.semaphore_signal(barrier, inc=1, device_id={"head": other}, device_id_type=MESH)
     for step in range(1, seq_count):
@@ -116,6 +109,14 @@
             device_id={"seq": lax.rem(seq + step, seq_count)},
             device_id_type=MESH,
         )
+    loads = [
+        pltpu.make_async_copy(conv_hbm.at[0], conv_w.at[0], load_sem.at[0]),
+        pltpu.make_async_copy(conv_hbm.at[1], conv_w.at[1], load_sem.at[1]),
+        pltpu.make_async_copy(qkv_hbm, qkv_w, load_sem.at[2]),
+    ]
+    for load in loads:
+        load.start()
+
     pl.semaphore_wait(barrier, seq_count)
 
     for piece in range(pieces):
@@ -244,12 +245,26 @@
     loads[1].wait()
     for part in range(PARTS):
         convolve(1, 2 * cells, part * span_rows, (part + 1) * span_rows)
-    pooled_all[head, seq] = jnp.mean(
+    own = inner_place * outer + outer_place
+    pooled_all[head, own] = jnp.mean(
         acc[...].reshape(pooled_rows, POOL, half), axis=1
     ).astype(BF16)
 
+    def in_order(step, act_on):
+        if step == 0:
+            act_on(outer_place)
+            return
+
+        @pl.when(outer_place - step >= 0)
+        def _():
+            act_on(outer_place - step)
+
+        @pl.when(outer_place + step < outer)
+        def _():
+            act_on(outer_place + step)
+
     def push(block, device, send, recv):
-        copy = pltpu.make_async_remote_copy(
+        return pltpu.make_async_remote_copy(
             src_ref=pooled_all.at[head, block],
             dst_ref=pooled_all.at[head, block],
             send_sem=send,
@@ -257,71 +272,113 @@
             device_id=device,
             device_id_type=MESH,
         )
-        copy.start()
-        return copy
+
+    def up(block):
+        target = lax.rem(outer_place + 1, outer) * inner + inner_place
+        return push(block, {"seq": target}, up_send.at[block], block_recv.at[block])
+
+    def down(block):
+        target = lax.rem(outer_place + outer - 1, outer) * inner + inner_place
+        return push(block, {"seq": target}, down_send.at[block], block_recv.at[block])
+
+    def aside(step, block):
+        target = outer_place * inner + lax.rem(inner_place + step, inner)
+        return push(block, {"seq": target}, aside_send.at[step - 1, block], block_recv.at[block])
+
+    def across(block):
+        return push(block, {"head": other}, core_send.at[block], core_recv.at[block])
 
     def arrived(block):
-        pltpu.make_async_remote_copy(
-            src_ref=pooled_all.at[head, block],
-            dst_ref=pooled_all.at[head, block],
-            send_sem=block_recv.at[block],
-            recv_sem=block_recv.at[block],
-            device_id={"head": other},
-            device_id_type=MESH,
-        ).wait_recv()
-
-    sent = []
-    for step in range(1, inner):
-        target = outer_place * inner + lax.rem(inner_place + step, inner)
-        sent.append(
-            push(seq, {"seq": target}, forward_send.at[step - 1], block_recv.at[seq])
-        )
-    for step in range(1, outer):
-        target = lax.rem(outer_place + step, outer) * inner + inner_place
-        sent.append(push(seq, {"seq": target}, own_send.at[step - 1], block_recv.at[seq]))
-    sent.append(push(seq, {"head": other}, core_send.at[0], core_recv.at[seq]))
-    count = 1
-    for step in range(1, outer):
-        block = lax.rem(outer_place + outer - step, outer) * inner + inner_place
-        arrived(block)
-        for aside in range(1, inner):
-            target = outer_place * inner + lax.rem(inner_place + aside, inner)
-            sent.append(
-                push(
-                    block,
-                    {"seq": target},
-                    forward_send.at[step * (inner - 1) + aside - 1],
-                    block_recv.at[block],
-                )
-            )
-        sent.append(push(block, {"head": other}, core_send.at[count], core_recv.at[block]))
-        count += 1
+        push(block, {"head": other}, core_send.at[block], block_recv.at[block]).wait_recv()
+
+    def column_block(place):
+        block = inner_place * outer + place
+
+        @pl.when(place != outer_place)
+        def _():
+            arrived(block)
+
+        @pl.when(jnp.logical_and(place <= outer_place, outer_place < outer - 1))
+        def _():
+            up(block).start()
+
+        @pl.when(jnp.logical_and(place >= outer_place, outer_place > 0))
+        def _():
+            down(block).start()
+
+        for step in range(1, inner):
+            aside(step, block).start()
+        across(block).start()
+
+    def aside_block(place):
+        for step in range(1, inner):
+            block = lax.rem(inner_place + inner - step, inner) * outer + place
+            arrived(block)
+            across(block).start()
+
+    def crossed(column):
+        for place in range(outer):
+            block = column * outer + place
+            pltpu.make_async_remote_copy(
+                src_ref=pooled_all.at[other, block],
+                dst_ref=pooled_all.at[other, block],
+                send_sem=core_send.at[block],
+                recv_sem=core_recv.at[block],
+                device_id={"head": other},
+                device_id_type=MESH,
+            ).wait_recv()
+
     for step in range(outer):
-        for aside in range(1, inner):
-            block = lax.rem(outer_place + outer - step, outer) * inner + lax.rem(
-                inner_place + inner - aside, inner
-            )
-            arrived(block)
-            sent.append(push(block, {"head": other}, core_send.at[count], core_recv.at[block]))
-            count += 1
-    for block in range(seq_count):
-        pltpu.make_async_remote_copy(
-            src_ref=pooled_all.at[other, block],
-            dst_ref=pooled_all.at[other, block],
-            send_sem=core_recv.at[block],
-            recv_sem=core_recv.at[block],
-            device_id={"head": other},
-            device_id_type=MESH,
-        ).wait_recv()
-
+        in_order(step, column_block)
     loads[2].wait()
     whole = seq_count * pooled_rows
     width = qkv_w.shape[2]
     stride = cells // POOL
     period = DILATION_FIRST // POOL
+    TILE = 256
+    BAND = outer * pooled_rows
+
+    def keys_values(column, between):
+        blocks = pl.ds(column * outer, outer)
+        place = pl.ds(pl.multiple_of(column * BAND, BAND), BAND)
+        done = 0
+        for kind, target in ((1, key_buf), (2, value_buf)):
+            for start in range(0, width, TILE):
+                columns = slice(start, start + TILE)
+                target[place, columns] = (
+                    jnp.dot(
+                        pooled_all[0, blocks].reshape(BAND, half),
+                        qkv_w[kind, :half, columns],
+                        preferred_element_type=F32,
+                    )
+                    + jnp.dot(
+                        pooled_all[1, blocks].reshape(BAND, half),
+                        qkv_w[kind, half:, columns],
+                        preferred_element_type=F32,
+                    )
+                ).astype(BF16)
+                between(done)
+                done += 1
+
+    tiles = 2 * (width // TILE)
+
+    def between(done):
+        for step in range(outer):
+            if done == min(2 * step, tiles - 1):
+                in_order(step, aside_block)
+
+    crossed(inner_place)
+    keys_values(inner_place, between)
+
+    @pl.loop(1, inner)
+    def _(step):
+        column = lax.rem(inner_place + step, inner)
+        crossed(column)
+        keys_values(column, lambda done: None)
 
     def position(place):
-        source = place // pooled_rows
+        block = place // pooled_rows
+        source = lax.rem(block, outer) * inner + block // outer
         within = lax.rem(place, pooled_rows)
         return within // stride * period + source * stride + lax.rem(within, stride)
 
@@ -332,29 +389,12 @@
     picked = [
         jnp.dot(pick, side, preferred_element_type=F32).astype(BF16) for side in sides
     ]
-    TILE = 256
     for column in range(0, width, TILE):
         columns = slice(column, column + TILE)
         query_buf[:, columns] = (
             jnp.dot(picked[0], qkv_w[0, :half, columns], preferred_element_type=F32)
             + jnp.dot(picked[1], qkv_w[0, half:, columns], preferred_element_type=F32)
         ).astype(BF16)
-
-    BAND = 8 * pooled_rows if seq_count % 8 == 0 else pooled_rows
-
-    @pl.loop(0, whole // BAND)
-    def _(band):
-        blocks = pl.ds(band * (BAND // pooled_rows), BAND // pooled_rows)
-        left = pooled_all[0, blocks].reshape(BAND, half)
-        right = pooled_all[1, blocks].reshape(BAND, half)
-        place = pl.ds(pl.multiple_of(band * BAND, BAND), BAND)
-        for kind, target in ((1, key_buf), (2, value_buf)):
-            for column in range(0, width, TILE):
-                columns = slice(column, column + TILE)
-                target[place, columns] = (
-                    jnp.dot(left, qkv_w[kind, :half, columns], preferred_element_type=F32)
-                    + jnp.dot(right, qkv_w[kind, half:, columns], preferred_element_type=F32)
-                ).astype(BF16)
 
     PAIR = 2 * HEAD_SIZE
     lane = lax.broadcasted_iota(jnp.int32, (pooled_rows, PAIR), 1)
@@ -400,8 +440,21 @@
     table_copy.wait_send()
     for copy in stream_copies:
         copy.wait_send()
-    for copy in sent:
-        copy.wait_send()
+    for place in range(outer):
+        block = inner_place * outer + place
+
+        @pl.when(jnp.logical_and(place <= outer_place, outer_place < outer - 1))
+        def _():
+            up(block).wait_send()
+
+        @pl.when(jnp.logical_and(place >= outer_place, outer_place > 0))
+        def _():
+            down(block).wait_send()
+
+        for step in range(1, inner):
+            aside(step, block).wait_send()
+    for block in range(seq_count):
+        across(block).wait_send()
 
 
 def local(byte_ids, embed_table, gains, conv_weight, conv_bias, qkv_weight):
@@ -444,8 +497,9 @@
             dma,
             dma((2,)),
             dma((2,)),
-            dma((max(outer - 1, 1),)),
-            dma((max(outer * (inner - 1), 1),)),
+            dma((seq_count,)),
+            dma((seq_count,)),
+            dma((max(inner - 1, 1), seq_count)),
             dma((seq_count,)),
             dma((seq_count,)),
             dma((seq_count,)),

time: 38.5 us -> 39.7 us (1.031)
  Pallas kernels: 36.6 us -> 37.9 us
    pallas_call x1, Pallas kernels: 36.6 us -> 37.9 us  [local(): pl.pallas_call(functools.partial(kernel, seq_count), out_shape=jax.ShapeD...]
where the time goes in v2:
time: 39.7 us; the launch traced here: 39.5 us
  Pallas kernels  37.9 us (95%)
  local copies, waits for them, and re-layouts  1.57 us (4%)
    pallas_call x1, Pallas kernels, local(): pl.pallas_call(functools.partial(kernel, seq_count), out_shape=jax.ShapeD...  37.9 us
    unnamed x1, local copies, waits for them, and re-layouts  1.57 us

profile of v2, /device:TPU:0, one launch (start us, length us, event | category | flops | bytes accessed | tf_op | source)
XLA Modules:
  0.0 39.5 jit_solution(3086450110836751872)
XLA Ops:
  0.0 37.9 %stem.1 = bf16[64,1024]{1,0:T(8,128)(2,1)} custom-call(s32[4,1,128]{2,1,0:T(1,128)} %bitcast.1, bf16[256,512]{1,0:T(8,128)(2,1)} %table_ref.1, f32[2,1024]{1,0:T(2,128)} %gains_ref.1, bf16[2,3,1024,512]{3,2,1,0:T(8,128)(2,1)} %conv_hbm.1, f32[2,512]{1,0:T(2,128)} %bias_ref.1, bf16[3,1024,1024]{2,1,0:T(8,128)(2,1)} %qkv_hbm.1), custom_call_target="tpu_custom_call" | custom-call | tf_op jit(solution)/shard_map/stem/pallas_call | solution.py:475
  37.9 1.6 %copy.8 = bf16[64,1024]{1,0:T(8,128)(2,1)} copy(bf16[64,1024]{1,0:T(8,128)(2,1)} %stem.1) | data formatting | bytes 262144

commit v3 on v2

--- a/solution.py
+++ b/solution.py
@@ -81,8 +81,7 @@
     table_recv,
     stream_send,
     stream_recv,
-    up_send,
-    down_send,
+    along_send,
     aside_send,
     core_send,
     block_recv,
@@ -165,7 +164,7 @@
         )
 
     CHUNK = 16
-    UNROLL = 2
+    UNROLL = 4
 
     @pl.loop(0, vocab // (CHUNK * UNROLL))
     def _(step):
@@ -273,13 +272,9 @@
             device_id_type=MESH,
         )
 
-    def up(block):
-        target = lax.rem(outer_place + 1, outer) * inner + inner_place
-        return push(block, {"seq": target}, up_send.at[block], block_recv.at[block])
-
-    def down(block):
-        target = lax.rem(outer_place + outer - 1, outer) * inner + inner_place
-        return push(block, {"seq": target}, down_send.at[block], block_recv.at[block])
+    def along(step):
+        target = lax.rem(outer_place + step, outer) * inner + inner_place
+        return push(own, {"seq": target}, along_send.at[step - 1], block_recv.at[own])
 
     def aside(step, block):
         target = outer_place * inner + lax.rem(inner_place + step, inner)
@@ -297,14 +292,6 @@
         @pl.when(place != outer_place)
         def _():
             arrived(block)
-
-        @pl.when(jnp.logical_and(place <= outer_place, outer_place < outer - 1))
-        def _():
-            up(block).start()
-
-        @pl.when(jnp.logical_and(place >= outer_place, outer_place > 0))
-        def _():
-            down(block).start()
 
         for step in range(1, inner):
             aside(step, block).start()
@@ -328,6 +315,8 @@
                 device_id_type=MESH,
             ).wait_recv()
 
+    for step in range(1, outer):
+        along(step).start()
     for step in range(outer):
         in_order(step, column_block)
     loads[2].wait()
@@ -443,16 +432,10 @@
     for place in range(outer):
         block = inner_place * outer + place
 
-        @pl.when(jnp.logical_and(place <= outer_place, outer_place < outer - 1))
-        def _():
-            up(block).wait_send()
-
-        @pl.when(jnp.logical_and(place >= outer_place, outer_place > 0))
-        def _():
-            down(block).wait_send()
-
         for step in range(1, inner):
             aside(step, block).wait_send()
+    for step in range(1, outer):
+        along(step).wait_send()
     for block in range(seq_count):
         across(block).wait_send()
 
@@ -497,8 +480,7 @@
             dma,
             dma((2,)),
             dma((2,)),
-            dma((seq_count,)),
-            dma((seq_count,)),
+            dma((max(outer - 1, 1),)),
             dma((max(inner - 1, 1), seq_count)),
             dma((seq_count,)),
             dma((seq_count,)),

time: 39.7 us -> 37.7 us (0.950)
  Pallas kernels: 37.9 us -> 35.6 us
    pallas_call x1, Pallas kernels: 37.9 us -> 35.6 us  [local(): pl.pallas_call(functools.partial(kernel, seq_count), out_shape=jax.ShapeD...]
where the time goes in v3:
time: 37.7 us; the launch traced here: 37.2 us
  Pallas kernels  35.6 us (94%)
  local copies, waits for them, and re-layouts  1.57 us (4%)
    pallas_call x1, Pallas kernels, local(): pl.pallas_call(functools.partial(kernel, seq_count), out_shape=jax.ShapeD...  35.6 us
    unnamed x1, local copies, waits for them, and re-layouts  1.57 us

profile of v3, /device:TPU:0, one launch (start us, length us, event | category | flops | bytes accessed | tf_op | source)
XLA Modules:
  0.0 37.2 jit_solution(9988754015063998420)
XLA Ops:
  0.0 35.6 %stem.1 = bf16[64,1024]{1,0:T(8,128)(2,1)} custom-call(s32[4,1,128]{2,1,0:T(1,128)} %bitcast.1, bf16[256,512]{1,0:T(8,128)(2,1)} %table_ref.1, f32[2,1024]{1,0:T(2,128)} %gains_ref.1, bf16[2,3,1024,512]{3,2,1,0:T(8,128)(2,1)} %conv_hbm.1, f32[2,512]{1,0:T(2,128)} %bias_ref.1, bf16[3,1024,1024]{2,1,0:T(8,128)(2,1)} %qkv_hbm.1), custom_call_target="tpu_custom_call" | custom-call | tf_op jit(solution)/shard_map/stem/pallas_call | solution.py:458
  35.6 1.6 %copy.8 = bf16[64,1024]{1,0:T(8,128)(2,1)} copy(bf16[64,1024]{1,0:T(8,128)(2,1)} %stem.1) | data formatting | bytes 262144
